TPU v7x, 32 devices: a whole 2x2x4 slice. The times are simulated.
32 devices in a mesh: dp: 16 (over z, y, x), seq: 2 (over core).
Axes of the slice: x: 2, y: 2, z: 4, core: 2. Of those that a mesh axis runs over, the one named last changes fastest.
Arguments:
- phonemes: bfloat16 [2, 32, 128, 512], P(None, None, 'dp'), may hold values from -60 to 60, as said below
- style_vector: bfloat16 [2, 32, 128], P(None, 'dp'), may hold values from -6 to 6
- frame_phone: int32 [2, 32, 1024], P(None, 'dp', 'seq'), may hold values from 0 to 127, as said below
- frame_count: int32 [2, 32], P(None, 'dp'), may hold values from 640 to 1024, as said below
- cotangent: bfloat16 [2, 32, 1024, 512], P(None, 'dp', 'seq'), may hold values from -6 to 6
- conv_master: float32 [3145728], P('dp'), may hold values from -0.15625 to 0.15625
- conv_moment: float32 [3145728], P('dp'), may hold values from -48 to 48
- conv_square: float32 [3145728], P('dp'), may hold values from 5.89824 to 23.59296
- bias_master: float32 [1024], P('dp'), may hold values from -2 to 2
- bias_moment: float32 [1024], P('dp'), may hold values from -80 to 80
- bias_square: float32 [1024], P('dp'), may hold values from 16.384 to 65.536
- style_master: float32 [524288], P('dp'), may hold values from -0.25 to 0.25
- style_moment: float32 [524288], P('dp'), may hold values from -80 to 80
- style_square: float32 [524288], P('dp'), may hold values from 16.384 to 65.536
- offset_master: float32 [4096], P('dp'), may hold values from -2 to 2
- offset_moment: float32 [4096], P('dp'), may hold values from -80 to 80
- offset_square: float32 [4096], P('dp'), may hold values from 16.384 to 65.536
Outputs:
- frames_out: float32 [2, 32, 1024, 512], P(None, 'dp', 'seq')
- phoneme_grad: float32 [2, 32, 128, 512], P(None, None, 'dp', 'seq')
- style_grad: float32 [2, 32, 128], P(None, 'dp')
- updated_conv: float32 [3145728], P('dp')
- moment_conv: float32 [3145728], P('dp')
- square_conv: float32 [3145728], P('dp')
- bfloat_conv: bfloat16 [3145728], P('dp')
- updated_bias: float32 [1024], P('dp')
- moment_bias: float32 [1024], P('dp')
- square_bias: float32 [1024], P('dp')
- bfloat_bias: bfloat16 [1024], P('dp')
- updated_style: float32 [524288], P('dp')
- moment_style: float32 [524288], P('dp')
- square_style: float32 [524288], P('dp')
- bfloat_style: bfloat16 [524288], P('dp')
- updated_offset: float32 [4096], P('dp')
- moment_offset: float32 [4096], P('dp')
- square_offset: float32 [4096], P('dp')
- bfloat_offset: bfloat16 [4096], P('dp')
Inputs may be any that keep to these rules, and one draw needn't show every extreme that they name: `phonemes`: phoneme features of order one, with varying scales. Frames from frame_count to 1023 of an item are padding. `frame_phone`: never falls along an item's frames.
All inputs are finite; a program needn't handle non-finite values.
Results may differ from a plain program's by a relative error of at most 0.014.
Values may be sent and summed in bfloat16 or wider, within the bound.
A program may use at most 192 MiB of HBM per device.

v0:
```python
from functools import reduce

import jax
import jax.numpy as jnp
from jax import lax
from jax.sharding import PartitionSpec as P

D = 512
S = 128
KERN = 3
LAYERS = 2
PH = 128
STEP = 10


NORM_EPS = 1e-05
HALF_ROOT = 0.7071067811865476
MOMENT_DECAY = 0.9
SQUARE_DECAY = 0.999
LEARN_RATE = 0.05
WEIGHT_DECAY = 0.01
ADAM_EPS = 1e-08


def padded(cells, sides, width):
    for axis, dim in sides:
        count = lax.axis_size(axis)
        ends = count - 1
        head = lax.slice_in_dim(cells, 0, width, axis=dim)
        tail = lax.slice_in_dim(cells, cells.shape[dim] - width, cells.shape[dim], axis=dim)
        cells = jnp.concatenate(
            [
                lax.ppermute(tail, axis, [(i, (i + 1) % count) for i in range(ends)]),
                cells,
                lax.ppermute(head, axis, [((i + 1) % count, i) for i in range(ends)]),
            ],
            axis=dim,
        )
    return cells


def shortened(shard):
    return jax.tree.map(lambda a: a.astype(jnp.bfloat16) if a.dtype == jnp.float32 else a, shard)


def unpack_weights(whole):
    return (
        whole[0].reshape(2 * LAYERS, KERN, D, D),
        whole[1].reshape(LAYERS, D),
        whole[2].reshape(2 * LAYERS, S, 2 * D),
        whole[3].reshape(2 * LAYERS, 2 * D),
    )


def adain_forward(values, valid, counted, style_rows, style_weight, offset_row):
    masked = values * valid
    sums = lax.psum((jnp.sum(masked, axis=1), jnp.sum(masked * values, axis=1)), "seq")
    mean_value = sums[0] / counted
    variance = sums[1] / counted - mean_value * mean_value
    inverse = lax.rsqrt(variance + NORM_EPS)
    params = jnp.dot(
        style_rows, style_weight, preferred_element_type=jnp.float32
    ) + offset_row.astype(jnp.float32)
    scale_part = params[:, :D]
    shift_part = params[:, D:]
    normed = (values - mean_value[:, None, :]) * inverse[:, None, :]
    shaped = (1.0 + scale_part[:, None, :]) * normed + shift_part[:, None, :]
    active = valid * jax.nn.silu(shaped)
    return (active.astype(jnp.bfloat16), (normed, shaped, inverse, scale_part))


def adain_backward(grad_active, cache, valid, counted, style_rows, style_weight):
    normed, shaped, inverse, scale_part = cache
    sigmoid_part = jax.nn.sigmoid(shaped)
    grad_shaped = grad_active * valid * sigmoid_part * (1.0 + shaped * (1.0 - sigmoid_part))
    sums = lax.psum((jnp.sum(grad_shaped, axis=1), jnp.sum(grad_shaped * normed, axis=1)), "seq")
    grad_shift = sums[0]
    grad_scale = sums[1]
    factor = (inverse * (1.0 + scale_part))[:, None, :]
    grad_values = (
        factor
        * (
            grad_shaped
            - (grad_shift[:, None, :] + normed * grad_scale[:, None, :]) / counted[:, :, None]
        )
        * valid
    )
    grad_params = jnp.concatenate([grad_scale, grad_shift], axis=1)
    weight_grad = 0.5 * jnp.dot(
        style_rows.astype(jnp.float32).T, grad_params, precision=lax.Precision.HIGHEST
    )
    offset_grad = 0.5 * jnp.sum(grad_params, axis=0)
    style_back = jnp.dot(
        grad_params, style_weight.astype(jnp.float32).T, precision=lax.Precision.HIGHEST
    )
    return (grad_values, weight_grad, offset_grad, style_back)


def conv_forward(active, weight_tensors):
    half = active.shape[1]
    padded_frames = padded(active, (("seq", 1),), 1)
    block_result = jnp.einsum(
        "ifc,cd->ifd",
        padded_frames[:, 0:half],
        weight_tensors[0],
        preferred_element_type=jnp.float32,
    )
    for kernel_tap_index in range(1, KERN):
        block_result = block_result + jnp.einsum(
            "ifc,cd->ifd",
            padded_frames[:, kernel_tap_index : kernel_tap_index + half],
            weight_tensors[kernel_tap_index],
            preferred_element_type=jnp.float32,
        )
    return (block_result, padded_frames)


def conv_backward(grad_low, padded_frames, weight_tensors):
    half = grad_low.shape[1]
    grad_padded = padded(grad_low, (("seq", 1),), 1)
    weight_grad = jnp.stack(
        [
            jnp.einsum(
                "ifc,ifd->cd",
                padded_frames[:, kernel_tap_index : kernel_tap_index + half],
                grad_low,
                preferred_element_type=jnp.float32,
            )
            for kernel_tap_index in range(KERN)
        ]
    )
    grad_input = jnp.einsum(
        "ifd,cd->ifc",
        grad_padded[:, KERN - 1 : KERN - 1 + half],
        weight_tensors[0],
        preferred_element_type=jnp.float32,
    )
    for kernel_tap_index in range(1, KERN):
        start = KERN - 1 - kernel_tap_index
        grad_input = grad_input + jnp.einsum(
            "ifd,cd->ifc",
            grad_padded[:, start : start + half],
            weight_tensors[kernel_tap_index],
            preferred_element_type=jnp.float32,
        )
    return (weight_grad, grad_input)


def micro_step(arrived, style_rows, phone, counts, cotan, params, frame_positions):
    conv_all, bias_all, style_all, offset_all = params
    valid = (frame_positions[None, :] < counts[:, None]).astype(jnp.float32)[:, :, None]
    counted = counts.astype(jnp.float32)[:, None]
    onehot = (phone[:, :, None] == jnp.arange(PH, dtype=jnp.int32)[None, None, :]).astype(
        jnp.bfloat16
    )
    hidden = jnp.einsum("ifp,ipd->ifd", onehot, arrived, preferred_element_type=jnp.float32) * valid
    caches = []
    for layer in range(LAYERS):
        first, cache_one = adain_forward(
            hidden, valid, counted, style_rows, style_all[2 * layer], offset_all[2 * layer]
        )
        middle, padded_one = conv_forward(first, conv_all[2 * layer])
        second, cache_two = adain_forward(
            middle, valid, counted, style_rows, style_all[2 * layer + 1], offset_all[2 * layer + 1]
        )
        branch, padded_two = conv_forward(second, conv_all[2 * layer + 1])
        branch = branch + bias_all[layer].astype(jnp.float32)
        caches.append((cache_one, padded_one, cache_two, padded_two))
        hidden = valid * (hidden + branch) * HALF_ROOT
    grad_hidden = cotan.astype(jnp.float32)
    conv_grads = [None] * (2 * LAYERS)
    bias_grads = [None] * LAYERS
    style_grads = [None] * (2 * LAYERS)
    offset_grads = [None] * (2 * LAYERS)
    style_back = jnp.zeros(style_rows.shape, jnp.float32)
    for layer in reversed(range(LAYERS)):
        cache_one, padded_one, cache_two, padded_two = caches[layer]
        grad_res = grad_hidden * valid * HALF_ROOT
        grad_low = grad_res.astype(jnp.bfloat16)
        conv_grads[2 * layer + 1], grad_second = conv_backward(
            grad_low, padded_two, conv_all[2 * layer + 1]
        )
        bias_grads[layer] = jnp.sum(grad_low, axis=(0, 1), dtype=jnp.float32)
        grad_middle, style_grads[2 * layer + 1], offset_grads[2 * layer + 1], extra_back = (
            adain_backward(
                grad_second, cache_two, valid, counted, style_rows, style_all[2 * layer + 1]
            )
        )
        style_back = style_back + extra_back
        conv_grads[2 * layer], grad_first = conv_backward(
            grad_middle.astype(jnp.bfloat16), padded_one, conv_all[2 * layer]
        )
        grad_input, style_grads[2 * layer], offset_grads[2 * layer], extra_back = adain_backward(
            grad_first, cache_one, valid, counted, style_rows, style_all[2 * layer]
        )
        style_back = style_back + extra_back
        grad_hidden = grad_res + grad_input
    phone_grad = jnp.einsum(
        "ifp,ifd->ipd", onehot, grad_hidden.astype(jnp.bfloat16), preferred_element_type=jnp.float32
    )
    weight_grads = (
        jnp.stack(conv_grads).reshape(-1),
        jnp.stack(bias_grads).reshape(-1),
        jnp.stack(style_grads).reshape(-1),
        jnp.stack(offset_grads).reshape(-1),
    )
    return (hidden, phone_grad, style_back, weight_grads)


def adamw_update(master, moment, square, gradient, step_value):
    new_moment = MOMENT_DECAY * moment + (1.0 - MOMENT_DECAY) * gradient
    new_square = SQUARE_DECAY * square + (1.0 - SQUARE_DECAY) * gradient * gradient
    first_fix = 1.0 - jnp.power(jnp.float32(MOMENT_DECAY), step_value)
    second_fix = 1.0 - jnp.power(jnp.float32(SQUARE_DECAY), step_value)
    updated = master - LEARN_RATE * (
        new_moment / first_fix / (jnp.sqrt(new_square / second_fix) + ADAM_EPS)
        + WEIGHT_DECAY * master
    )
    return (updated, new_moment, new_square, updated.astype(jnp.bfloat16))


def on_device(
    phonemes,
    style_vector,
    frame_phone,
    frame_count,
    cotangent,
    conv_master,
    conv_moment,
    conv_square,
    bias_master,
    bias_moment,
    bias_square,
    style_master,
    style_moment,
    style_square,
    offset_master,
    offset_moment,
    offset_square,
):
    micros = cotangent.shape[0]
    half_frames = cotangent.shape[2]
    frame_positions = lax.axis_index("seq") * half_frames + jnp.arange(half_frames, dtype=jnp.int32)
    masters = (conv_master, bias_master, style_master, offset_master)
    device_shards = tuple((master.astype(jnp.bfloat16) for master in masters))
    frames_list = []
    phone_list = []
    style_list = []
    grad_list = []
    for micro_index in range(micros):
        params = unpack_weights(
            (
                lax.all_gather(device_shards[0], "dp", axis=0, tiled=True),
                lax.all_gather(device_shards[1], "dp", axis=0, tiled=True),
                lax.all_gather(device_shards[2], "dp", axis=0, tiled=True),
                lax.all_gather(device_shards[3], "dp", axis=0, tiled=True),
            )
        )
        arrived = lax.all_to_all(
            phonemes[micro_index], "dp", split_axis=0, concat_axis=1, tiled=True
        )
        output, phone_grad, style_back, weight_grads = micro_step(
            arrived,
            style_vector[micro_index],
            frame_phone[micro_index],
            frame_count[micro_index],
            cotangent[micro_index],
            params,
            frame_positions,
        )
        frames_list.append(output)
        style_list.append(style_back)
        phone_part = lax.psum_scatter(
            phone_grad.astype(jnp.bfloat16), "seq", scatter_dimension=2, tiled=True
        ).astype(jnp.float32)
        phone_list.append(
            lax.all_to_all(
                phone_part.astype(jnp.bfloat16), "dp", split_axis=1, concat_axis=0, tiled=True
            ).astype(phone_part.dtype)
        )
        grad_list.append(
            (
                lax.psum_scatter(weight_grads[0], "dp", scatter_dimension=0, tiled=True),
                lax.psum_scatter(weight_grads[1], "dp", scatter_dimension=0, tiled=True),
                lax.psum_scatter(weight_grads[2], "dp", scatter_dimension=0, tiled=True),
                lax.psum_scatter(weight_grads[3], "dp", scatter_dimension=0, tiled=True),
            )
        )
    summed = tuple((reduce(jnp.add, members) for members in zip(*grad_list)))
    summed = jax.tree.map(lambda part: part.astype(jnp.float32), lax.psum(shortened(summed), "seq"))
    phone_grads = jnp.stack(phone_list)
    step_value = jnp.float32(STEP)
    conv_out = adamw_update(conv_master, conv_moment, conv_square, summed[0], step_value)
    bias_out = adamw_update(bias_master, bias_moment, bias_square, summed[1], step_value)
    style_out = adamw_update(style_master, style_moment, style_square, summed[2], step_value)
    offset_out = adamw_update(offset_master, offset_moment, offset_square, summed[3], step_value)
    return (
        jnp.stack(frames_list),
        phone_grads,
        jnp.stack(style_list),
        conv_out[0],
        conv_out[1],
        conv_out[2],
        conv_out[3],
        bias_out[0],
        bias_out[1],
        bias_out[2],
        bias_out[3],
        style_out[0],
        style_out[1],
        style_out[2],
        style_out[3],
        offset_out[0],
        offset_out[1],
        offset_out[2],
        offset_out[3],
    )


def solution(mesh):
    return jax.shard_map(
        on_device,
        mesh=mesh,
        in_specs=(
            P(None, None, "dp", None),
            P(None, "dp", None),
            P(None, "dp", "seq"),
            P(None, "dp"),
            P(None, "dp", "seq", None),
            P("dp"),
            P("dp"),
            P("dp"),
            P("dp"),
            P("dp"),
            P("dp"),
            P("dp"),
            P("dp"),
            P("dp"),
            P("dp"),
            P("dp"),
            P("dp"),
        ),
        out_specs=(
            P(None, "dp", "seq", None),
            P(None, None, "dp", "seq"),
            P(None, "dp", None),
            P("dp"),
            P("dp"),
            P("dp"),
            P("dp"),
            P("dp"),
            P("dp"),
            P("dp"),
            P("dp"),
            P("dp"),
            P("dp"),
            P("dp"),
            P("dp"),
            P("dp"),
            P("dp"),
            P("dp"),
            P("dp"),
        ),
        check_vma=False,
    )
```

profile of v0, /device:TPU:0, one launch (start us, length us, event | category | flops | bytes accessed | tf_op | source)
XLA Modules:
  0.0 1162.6 jit_solution(6042191141755055294)
XLA Ops:
  11.8 8.3 all-to-all-start.1
  24.4 42.4 %all-reduce = bf16[1024]{0:T(1024)(128)(2,1)S(1)} all-reduce(bf16[1024]{0:T(1024)(128)(2,1)S(1)} %dynamic-update-slice), channel_id=1, replica_groups=mesh['dp'=16,'seq'=2] {'dp'}, use_global_device_ids=true, to_apply=%add | all-reduce | flops 1024 | bytes 4096
  66.8 35.6 %all-gather = bf16[16,1,256]{2,1,0:T(2,128)(2,1)S(1)} all-gather(bf16[1,1,256]{2,1,0:T(2,128)(2,1)S(1)} %reshape.543), channel_id=1, replica_groups=mesh['dp'=16,'seq'=2] {'dp'}, dimensions={0}, use_global_device_ids=true | all-gather | bytes 8704 | tf_op jit(solution)/shard_map/all_gather | solution.py:256
  102.5 3.5 all-to-all-start
  108.1 10.0 all-to-all-done
  118.7 3.3 all-reduce.13
  130.8 3.0 collective-permute-start.8
  137.9 3.0 collective-permute-start
  141.8 26.5 %all-gather.6.cloned.1.call-done = bf16[3145728]{0:T(1024)(128)(2,1)} async-done(((bf16[196608]{0:T(1024)(128)(2,1)}), bf16[3145728]{0:T(1024)(128)(2,1)}) %all-gather.6.cloned.1.call-update) | async-done | bytes 6291472 | tf_op jit(solution)/shard_map/all_gather | solution.py:253
  168.3 5.0 fusion.206
  179.2 3.4 fusion.4
  187.1 3.5 all-reduce.12
  190.7 4.9 convert_reduce_fusion.2
  204.8 3.5 fusion.237
  219.8 3.0 collective-permute-start.2
  235.0 3.4 multiply_reduce_fusion.14
  243.0 4.3 all-reduce.11
  261.2 3.1 collective-permute-start.4
  270.5 3.3 all-reduce.10
  274.0 5.4 fusion.190
  283.0 3.8 all-reduce.9
  286.9 3.6 multiply_convert_fusion.1
  331.4 3.0 collective-permute-start.27
  336.8 3.1 fusion.189
  339.8 3.2 collective-permute-start.19
  343.8 3.1 fusion.185
  346.9 3.5 all-reduce.8
  350.3 4.5 convert_reduce_fusion.1
  407.3 4.2 fusion.188
  413.1 3.4 fusion.184
  416.4 4.2 all-reduce.7
  420.7 3.5 multiply_convert_fusion
  438.2 3.0 collective-permute-start.23
  452.7 5.9 maximum_add_fusion
  458.6 6.8 copy.156
  467.1 3.0 fusion.187
  471.7 3.1 fusion.183
  474.8 4.2 all-reduce.6
  481.9 4.7 convolution_convert_fusion
  486.8 3.4 maximum_add_fusion.1
  493.1 3.4 copy.158
  496.6 606.5 %all-reduce.20 = (bf16[3145728]{0:T(1024)(128)(2,1)}, bf16[1024]{0:T(1024)(128)(2,1)S(1)}, bf16[524288]{0:T(1024)(128)(2,1)}, bf16[4096]{0:T(1024)(128)(2,1)S(1)}) all-reduce(f32[3145728]{0:T(1024)} %bitcast.372, f32[1024]{0:T(1024)S(1)} %bitcast.391, f32[524288]{0:T(1024)} %bitcast.374, ...), channel_id=8, replica_groups=mesh['dp'=16,'seq'=2] {'dp'}, use_global_device_ids=true, to_apply=%region_66.67.clone | all-reduce | flops 3675136 | bytes 22050816
  1107.2 4.1 convolution_convert_fusion.1
  1117.4 6.9 all-to-all-start.3
  1127.1 3.5 fusion.199
  1130.6 8.1 reduce-scatter.3.cloned.1.call-done
  1140.3 6.8 all-to-all-start.2
  1148.0 7.1 all-to-all-done.2
  (630 shorter events, 240.7 us)
Async XLA Ops:
  7.2 95.2 %copy-start.145 = (s32[2,2,512]{2,1,0:T(2,128)S(1)}, s32[2,2,512]{2,1,0:T(2,128)}, u32[]{:S(2)}) copy-start(s32[2,2,512]{2,1,0:T(2,128)} %param.19) | copy-start | bytes 24580
  7.3 114.8 %all-gather.4.cloned.1.call-start = ((), (), s32[]{:S(2)}) async-start(), calls=%async_computation.6 | async-start | bytes 1114112 | tf_op jit(solution)/shard_map/all_gather | solution.py:255
  8.9 159.4 %all-gather.6.cloned.1.call-start = ((), (), s32[]{:S(2)}) async-start(), calls=%async_computation.7 | async-start | bytes 6684672 | tf_op jit(solution)/shard_map/all_gather | solution.py:253
  11.8 90.7 %all-to-all-start.1 = ((bf16[32,8,512]{2,1,0:T(8,128)(2,1)}), bf16[32,8,512]{2,1,0:T(8,128)(2,1)S(1)}, u32[]{:S(2)}, u32[]{:S(2)}) async-start(bf16[32,8,512]{2,1,0:T(8,128)(2,1)} %get-tuple-element.196), calls=%async_computation.1 | async-start | bytes 524288 | tf_op jit(solution)/shard_map/all_to_all | solution.py:259
  102.5 15.6 %all-to-all-start = ((bf16[32,8,512]{2,1,0:T(8,128)(2,1)}), bf16[32,8,512]{2,1,0:T(8,128)(2,1)S(1)}, u32[]{:S(2)}, u32[]{:S(2)}) async-start(bf16[32,8,512]{2,1,0:T(8,128)(2,1)} %get-tuple-element.195), calls=%async_computation | async-start | bytes 524288 | tf_op jit(solution)/shard_map/all_to_all | solution.py:259
  106.0 1009.6 %reduce-scatter.5.cloned.1.call-start = ((), (), s32[]{:S(2)}) async-start(), calls=%async_computation.9 | async-start | bytes 393216 | tf_op jit(solution)/shard_map/reduce_scatter | solution.py:273
  129.3 49.9 %copy-start.9 = (bf16[2,512,512]{2,1,0:T(8,128)(2,1)}, bf16[2,512,512]{2,1,0:T(8,128)(2,1)S(1)}, u32[]{:S(2)}) copy-start(bf16[2,512,512]{2,1,0:T(8,128)(2,1)S(1)} %multiply_convert_fusion.7) | copy-start | bytes 3145732
  129.3 49.8 %collective-permute-start.9 = (bf16[2,1,512]{2,1,0:T(2,128)(2,1)S(1)}, bf16[2,1,512]{2,1,0:T(2,128)(2,1)S(1)}, u32[]{:S(2)}, u32[]{:S(2)}) collective-permute-start(bf16[2,1,512]{2,1,0:T(2,128)(2,1)S(1)} %get-tuple-element.193), channel_id=1, source_target_pairs={{1,0},{3,2},{5,4},{7,6},{9,8},{11,10},{13,12},{15,14},{17,16},{19,... | collective-permute-start | bytes 6152 | tf_op jit(solution)/shard_map/ppermute | solution.py:35
  130.8 45.2 %collective-permute-start.8 = (bf16[2,1,512]{2,1,0:T(2,128)(2,1)S(1)}, bf16[2,1,512]{2,1,0:T(2,128)(2,1)S(1)}, u32[]{:S(2)}, u32[]{:S(2)}) collective-permute-start(bf16[2,1,512]{2,1,0:T(2,128)(2,1)S(1)} %get-tuple-element.194), channel_id=1, source_target_pairs={{0,1},{2,3},{4,5},{6,7},{8,9},{10,11},{12,13},{14,15},{16,17},{18,... | collective-permute-start | bytes 6152 | tf_op jit(solution)/shard_map/ppermute | solution.py:33
  136.6 48.2 %collective-permute-start.1 = (bf16[2,1,512]{2,1,0:T(2,128)(2,1)S(1)}, bf16[2,1,512]{2,1,0:T(2,128)(2,1)S(1)}, u32[]{:S(2)}, u32[]{:S(2)}) collective-permute-start(bf16[2,1,512]{2,1,0:T(2,128)(2,1)S(1)} %get-tuple-element.191), channel_id=1, source_target_pairs={{1,0},{3,2},{5,4},{7,6},{9,8},{11,10},{13,12},{15,14},{17,16},{19,... | collective-permute-start | bytes 6152 | tf_op jit(solution)/shard_map/ppermute | solution.py:35
  137.9 45.5 %collective-permute-start = (bf16[2,1,512]{2,1,0:T(2,128)(2,1)S(1)}, bf16[2,1,512]{2,1,0:T(2,128)(2,1)S(1)}, u32[]{:S(2)}, u32[]{:S(2)}) collective-permute-start(bf16[2,1,512]{2,1,0:T(2,128)(2,1)S(1)} %get-tuple-element.192), channel_id=1, source_target_pairs={{0,1},{2,3},{4,5},{6,7},{8,9},{10,11},{12,13},{14,15},{16,17},{18,... | collective-permute-start | bytes 6152 | tf_op jit(solution)/shard_map/ppermute | solution.py:33
  195.6 35.5 %copy-start.20 = (bf16[2,512,512]{2,1,0:T(8,128)(2,1)}, bf16[2,512,512]{2,1,0:T(8,128)(2,1)S(1)}, u32[]{:S(2)}) copy-start(bf16[2,512,512]{2,1,0:T(8,128)(2,1)S(1)} %get-tuple-element.219) | copy-start | bytes 3145732
  201.5 28.4 %collective-permute-start.10 = (bf16[2,1,512]{2,1,0:T(2,128)(2,1)S(1)}, bf16[2,1,512]{2,1,0:T(2,128)(2,1)S(1)}, u32[]{:S(2)}, u32[]{:S(2)}) collective-permute-start(bf16[2,1,512]{2,1,0:T(2,128)(2,1)S(1)} %get-tuple-element.190), channel_id=1, source_target_pairs={{0,1},{2,3},{4,5},{6,7},{8,9},{10,11},{12,13},{14,15},{16,17},{18,... | collective-permute-start | bytes 6152 | tf_op jit(solution)/shard_map/ppermute | solution.py:33
  215.8 16.1 %collective-permute-start.11 = (bf16[2,1,512]{2,1,0:T(2,128)(2,1)S(1)}, bf16[2,1,512]{2,1,0:T(2,128)(2,1)S(1)}, u32[]{:S(2)}, u32[]{:S(2)}) collective-permute-start(bf16[2,1,512]{2,1,0:T(2,128)(2,1)S(1)} %get-tuple-element.189), channel_id=1, source_target_pairs={{1,0},{3,2},{5,4},{7,6},{9,8},{11,10},{13,12},{15,14},{17,16},{19,... | collective-permute-start | bytes 6152 | tf_op jit(solution)/shard_map/ppermute | solution.py:35
  218.5 22.1 %collective-permute-start.3 = (bf16[2,1,512]{2,1,0:T(2,128)(2,1)S(1)}, bf16[2,1,512]{2,1,0:T(2,128)(2,1)S(1)}, u32[]{:S(2)}, u32[]{:S(2)}) collective-permute-start(bf16[2,1,512]{2,1,0:T(2,128)(2,1)S(1)} %get-tuple-element.187), channel_id=1, source_target_pairs={{1,0},{3,2},{5,4},{7,6},{9,8},{11,10},{13,12},{15,14},{17,16},{19,... | collective-permute-start | bytes 6152 | tf_op jit(solution)/shard_map/ppermute | solution.py:35
  219.8 18.6 %collective-permute-start.2 = (bf16[2,1,512]{2,1,0:T(2,128)(2,1)S(1)}, bf16[2,1,512]{2,1,0:T(2,128)(2,1)S(1)}, u32[]{:S(2)}, u32[]{:S(2)}) collective-permute-start(bf16[2,1,512]{2,1,0:T(2,128)(2,1)S(1)} %get-tuple-element.188), channel_id=1, source_target_pairs={{0,1},{2,3},{4,5},{6,7},{8,9},{10,11},{12,13},{14,15},{16,17},{18,... | collective-permute-start | bytes 6152 | tf_op jit(solution)/shard_map/ppermute | solution.py:33
  228.3 45.6 %collective-permute-start.25 = (bf16[2,1,512]{2,1,0:T(2,128)(2,1)S(1)}, bf16[2,1,512]{2,1,0:T(2,128)(2,1)S(1)}, u32[]{:S(2)}, u32[]{:S(2)}) collective-permute-start(bf16[2,1,512]{2,1,0:T(2,128)(2,1)S(1)} %get-tuple-element.173), channel_id=1, source_target_pairs={{0,1},{2,3},{4,5},{6,7},{8,9},{10,11},{12,13},{14,15},{16,17},{18,... | collective-permute-start | bytes 6152 | tf_op jit(solution)/shard_map/ppermute | solution.py:33
  229.9 23.4 %collective-permute-start.24 = (bf16[2,1,512]{2,1,0:T(2,128)(2,1)S(1)}, bf16[2,1,512]{2,1,0:T(2,128)(2,1)S(1)}, u32[]{:S(2)}, u32[]{:S(2)}) collective-permute-start(bf16[2,1,512]{2,1,0:T(2,128)(2,1)S(1)} %get-tuple-element.174), channel_id=1, source_target_pairs={{1,0},{3,2},{5,4},{7,6},{9,8},{11,10},{13,12},{15,14},{17,16},{19,... | collective-permute-start | bytes 6152 | tf_op jit(solution)/shard_map/ppermute | solution.py:35
  231.9 47.6 %collective-permute-start.17 = (bf16[2,1,512]{2,1,0:T(2,128)(2,1)S(1)}, bf16[2,1,512]{2,1,0:T(2,128)(2,1)S(1)}, u32[]{:S(2)}, u32[]{:S(2)}) collective-permute-start(bf16[2,1,512]{2,1,0:T(2,128)(2,1)S(1)} %get-tuple-element.171), channel_id=1, source_target_pairs={{0,1},{2,3},{4,5},{6,7},{8,9},{10,11},{12,13},{14,15},{16,17},{18,... | collective-permute-start | bytes 6152 | tf_op jit(solution)/shard_map/ppermute | solution.py:33
  238.4 19.4 %collective-permute-start.16 = (bf16[2,1,512]{2,1,0:T(2,128)(2,1)S(1)}, bf16[2,1,512]{2,1,0:T(2,128)(2,1)S(1)}, u32[]{:S(2)}, u32[]{:S(2)}) collective-permute-start(bf16[2,1,512]{2,1,0:T(2,128)(2,1)S(1)} %get-tuple-element.172), channel_id=1, source_target_pairs={{1,0},{3,2},{5,4},{7,6},{9,8},{11,10},{13,12},{15,14},{17,16},{19,... | collective-permute-start | bytes 6152 | tf_op jit(solution)/shard_map/ppermute | solution.py:35
  248.4 12.9 %collective-permute-start.12 = (bf16[2,1,512]{2,1,0:T(2,128)(2,1)S(1)}, bf16[2,1,512]{2,1,0:T(2,128)(2,1)S(1)}, u32[]{:S(2)}, u32[]{:S(2)}) collective-permute-start(bf16[2,1,512]{2,1,0:T(2,128)(2,1)S(1)} %get-tuple-element.186), channel_id=1, source_target_pairs={{0,1},{2,3},{4,5},{6,7},{8,9},{10,11},{12,13},{14,15},{16,17},{18,... | collective-permute-start | bytes 6152 | tf_op jit(solution)/shard_map/ppermute | solution.py:33
  256.4 8.7 collective-permute-start.13
  257.9 10.3 collective-permute-start.5
  261.2 6.2 collective-permute-start.4
  311.5 61.3 %collective-permute-start.14 = (bf16[2,1,512]{2,1,0:T(2,128)(2,1)}, bf16[2,1,512]{2,1,0:T(2,128)(2,1)}, u32[]{:S(2)}, u32[]{:S(2)}) collective-permute-start(bf16[2,1,512]{2,1,0:T(2,128)(2,1)} %get-tuple-element.178), channel_id=1, source_target_pairs={{0,1},{2,3},{4,5},{6,7},{8,9},{10,11},{12,13},{14,15},{16,17},{18,... | collective-permute-start | bytes 6152 | tf_op jit(solution)/shard_map/ppermute | solution.py:33
  314.3 67.5 %collective-permute-start.6 = (bf16[2,1,512]{2,1,0:T(2,128)(2,1)}, bf16[2,1,512]{2,1,0:T(2,128)(2,1)}, u32[]{:S(2)}, u32[]{:S(2)}) collective-permute-start(bf16[2,1,512]{2,1,0:T(2,128)(2,1)} %get-tuple-element.176), channel_id=1, source_target_pairs={{0,1},{2,3},{4,5},{6,7},{8,9},{10,11},{12,13},{14,15},{16,17},{18,... | collective-permute-start | bytes 6152 | tf_op jit(solution)/shard_map/ppermute | solution.py:33
  316.1 68.7 %collective-permute-start.7 = (bf16[2,1,512]{2,1,0:T(2,128)(2,1)}, bf16[2,1,512]{2,1,0:T(2,128)(2,1)S(1)}, u32[]{:S(2)}, u32[]{:S(2)}) collective-permute-start(bf16[2,1,512]{2,1,0:T(2,128)(2,1)} %get-tuple-element.175), channel_id=1, source_target_pairs={{1,0},{3,2},{5,4},{7,6},{9,8},{11,10},{13,12},{15,14},{17,16},{19,... | collective-permute-start | bytes 6152 | tf_op jit(solution)/shard_map/ppermute | solution.py:35
  317.4 14.0 %collective-permute-start.26 = (bf16[2,1,512]{2,1,0:T(2,128)(2,1)S(1)}, bf16[2,1,512]{2,1,0:T(2,128)(2,1)S(1)}, u32[]{:S(2)}, u32[]{:S(2)}) collective-permute-start(bf16[2,1,512]{2,1,0:T(2,128)(2,1)S(1)} %get-tuple-element.170), channel_id=1, source_target_pairs={{1,0},{3,2},{5,4},{7,6},{9,8},{11,10},{13,12},{15,14},{17,16},{19,... | collective-permute-start | bytes 6152 | tf_op jit(solution)/shard_map/ppermute | solution.py:35
  330.1 47.4 %collective-permute-start.15 = (bf16[2,1,512]{2,1,0:T(2,128)(2,1)}, bf16[2,1,512]{2,1,0:T(2,128)(2,1)S(1)}, u32[]{:S(2)}, u32[]{:S(2)}) collective-permute-start(bf16[2,1,512]{2,1,0:T(2,128)(2,1)} %get-tuple-element.177), channel_id=1, source_target_pairs={{1,0},{3,2},{5,4},{7,6},{9,8},{11,10},{13,12},{15,14},{17,16},{19,... | collective-permute-start | bytes 6152 | tf_op jit(solution)/shard_map/ppermute | solution.py:35
  331.4 3.9 collective-permute-start.27
  335.3 4.6 collective-permute-start.18
  339.8 4.0 collective-permute-start.19
  367.6 38.7 %collective-permute-start.29 = (bf16[2,1,512]{2,1,0:T(2,128)(2,1)}, bf16[2,1,512]{2,1,0:T(2,128)(2,1)}, u32[]{:S(2)}, u32[]{:S(2)}) collective-permute-start(bf16[2,1,512]{2,1,0:T(2,128)(2,1)} %get-tuple-element.165), channel_id=1, source_target_pairs={{0,1},{2,3},{4,5},{6,7},{8,9},{10,11},{12,13},{14,15},{16,17},{18,... | collective-permute-start | bytes 6152 | tf_op jit(solution)/shard_map/ppermute | solution.py:33
  372.9 32.7 %collective-permute-start.28 = (bf16[2,1,512]{2,1,0:T(2,128)(2,1)}, bf16[2,1,512]{2,1,0:T(2,128)(2,1)S(1)}, u32[]{:S(2)}, u32[]{:S(2)}) collective-permute-start(bf16[2,1,512]{2,1,0:T(2,128)(2,1)} %get-tuple-element.166), channel_id=1, source_target_pairs={{1,0},{3,2},{5,4},{7,6},{9,8},{11,10},{13,12},{15,14},{17,16},{19,... | collective-permute-start | bytes 6152 | tf_op jit(solution)/shard_map/ppermute | solution.py:35
  377.5 34.8 %collective-permute-start.21 = (bf16[2,1,512]{2,1,0:T(2,128)(2,1)S(1)}, bf16[2,1,512]{2,1,0:T(2,128)(2,1)S(1)}, u32[]{:S(2)}, u32[]{:S(2)}) collective-permute-start(bf16[2,1,512]{2,1,0:T(2,128)(2,1)S(1)} %copy-done.155), channel_id=1, source_target_pairs={{0,1},{2,3},{4,5},{6,7},{8,9},{10,11},{12,13},{14,15},{16,17},{18,... | collective-permute-start | bytes 6152 | tf_op jit(solution)/shard_map/ppermute | solution.py:33
  381.7 29.7 %collective-permute-start.20 = (bf16[2,1,512]{2,1,0:T(2,128)(2,1)S(1)}, bf16[2,1,512]{2,1,0:T(2,128)(2,1)S(1)}, u32[]{:S(2)}, u32[]{:S(2)}) collective-permute-start(bf16[2,1,512]{2,1,0:T(2,128)(2,1)S(1)} %copy-done.156), channel_id=1, source_target_pairs={{1,0},{3,2},{5,4},{7,6},{9,8},{11,10},{13,12},{15,14},{17,16},{19,... | collective-permute-start | bytes 6152 | tf_op jit(solution)/shard_map/ppermute | solution.py:35
  434.8 31.5 %collective-permute-start.31 = (bf16[2,1,512]{2,1,0:T(2,128)(2,1)S(1)}, bf16[2,1,512]{2,1,0:T(2,128)(2,1)S(1)}, u32[]{:S(2)}, u32[]{:S(2)}) collective-permute-start(bf16[2,1,512]{2,1,0:T(2,128)(2,1)S(1)} %get-tuple-element.161), channel_id=1, source_target_pairs={{0,1},{2,3},{4,5},{6,7},{8,9},{10,11},{12,13},{14,15},{16,17},{18,... | collective-permute-start | bytes 6152 | tf_op jit(solution)/shard_map/ppermute | solution.py:33
  436.9 28.6 %collective-permute-start.30 = (bf16[2,1,512]{2,1,0:T(2,128)(2,1)S(1)}, bf16[2,1,512]{2,1,0:T(2,128)(2,1)S(1)}, u32[]{:S(2)}, u32[]{:S(2)}) collective-permute-start(bf16[2,1,512]{2,1,0:T(2,128)(2,1)S(1)} %get-tuple-element.162), channel_id=1, source_target_pairs={{1,0},{3,2},{5,4},{7,6},{9,8},{11,10},{13,12},{15,14},{17,16},{19,... | collective-permute-start | bytes 6152 | tf_op jit(solution)/shard_map/ppermute | solution.py:35
  438.2 32.8 %collective-permute-start.23 = (bf16[2,1,512]{2,1,0:T(2,128)(2,1)S(1)}, bf16[2,1,512]{2,1,0:T(2,128)(2,1)S(1)}, u32[]{:S(2)}, u32[]{:S(2)}) collective-permute-start(bf16[2,1,512]{2,1,0:T(2,128)(2,1)S(1)} %get-tuple-element.159), channel_id=1, source_target_pairs={{0,1},{2,3},{4,5},{6,7},{8,9},{10,11},{12,13},{14,15},{16,17},{18,... | collective-permute-start | bytes 6152 | tf_op jit(solution)/shard_map/ppermute | solution.py:33
  441.2 29.0 %collective-permute-start.22 = (bf16[2,1,512]{2,1,0:T(2,128)(2,1)S(1)}, bf16[2,1,512]{2,1,0:T(2,128)(2,1)S(1)}, u32[]{:S(2)}, u32[]{:S(2)}) collective-permute-start(bf16[2,1,512]{2,1,0:T(2,128)(2,1)S(1)} %get-tuple-element.160), channel_id=1, source_target_pairs={{1,0},{3,2},{5,4},{7,6},{9,8},{11,10},{13,12},{15,14},{17,16},{19,... | collective-permute-start | bytes 6152 | tf_op jit(solution)/shard_map/ppermute | solution.py:35
  486.7 640.4 %all-reduce.19.cloned.1.call-start = ((), (), s32[]{:S(2)}) async-start(), calls=%async_computation.10 | async-start | bytes 917504 | tf_op jit(solution)/shard_map/psum | solution.py:290
  496.6 609.8 %copy-start.84 = (bf16[128,1024]{1,0:T(8,128)(2,1)S(1)}, bf16[128,1024]{1,0:T(8,128)(2,1)}, u32[]{:S(2)}) copy-start(bf16[128,1024]{1,0:T(8,128)(2,1)} %copy-done.83) | copy-start | bytes 786436
  496.6 610.5 %copy-start.149 = (f32[2,512]{1,0:T(2,128)S(1)}, f32[2,512]{1,0:T(2,128)}, u32[]{:S(2)}) copy-start(f32[2,512]{1,0:T(2,128)} %get-tuple-element.117) | copy-start | bytes 12292
  496.6 610.5 %copy-start.152 = (s32[2,512]{1,0:T(2,128)S(1)}, s32[2,512]{1,0:T(2,128)}, u32[]{:S(2)}) copy-start(s32[2,512]{1,0:T(2,128)} %copy-done.151) | copy-start | bytes 12292
  1107.1 31.6 %reduce-scatter.3.cloned.1.call-start = ((), (), s32[]{:S(2)}) async-start(), calls=%async_computation.8 | async-start | bytes 393216 | tf_op jit(solution)/shard_map/reduce_scatter | solution.py:273
  1117.4 22.9 %all-to-all-start.3 = ((bf16[2,128,256]{2,0,1:T(2,128)(2,1)}), bf16[2,128,256]{2,0,1:T(2,128)(2,1)S(1)}, u32[]{:S(2)}, u32[]{:S(2)}) async-start(bf16[2,128,256]{2,0,1:T(2,128)(2,1)} %copy.103), calls=%async_computation.5 | async-start | bytes 262144 | tf_op jit(solution)/shard_map/all_to_all | solution.py:277
  1127.1 20.0 %copy-start.128 = (bf16[32768]{0:T(1024)(128)(2,1)S(1)}, bf16[32768]{0:T(1024)(128)(2,1)}, u32[]{:S(2)}) copy-start(bf16[32768]{0:T(1024)(128)(2,1)} %get-tuple-element.90) | copy-start | bytes 196612
  1140.3 14.7 %all-to-all-start.2 = ((bf16[2,128,256]{2,0,1:T(2,128)(2,1)}), bf16[2,128,256]{2,0,1:T(2,128)(2,1)S(1)}, u32[]{:S(2)}, u32[]{:S(2)}) async-start(bf16[2,128,256]{2,0,1:T(2,128)(2,1)} %copy.101), calls=%async_computation.3 | async-start | bytes 262144 | tf_op jit(solution)/shard_map/all_to_all | solution.py:277
  (168 other events, 946.0 us)
Sparse Core Ops, SparseCore 0:
  11.4 58.7 all-gather.3
  73.6 94.7 all-gather.5
  486.8 5.9 reduce-scatter.4
  1107.2 19.8 all-reduce.18
  1129.7 8.8 reduce-scatter.2
where the time goes:
time: 1170 us; the launch traced here: 1160 us
  blocking collectives  717 us (61%)
  matrix products  152 us (13%)
  starting transfers between devices  90.5 us (8%)
  local copies, waits for them, and re-layouts  64 us (5%)
  other arithmetic  63.8 us (5%)
  waiting for transfers between devices  54.8 us (5%)
  between operations  20 us (2%)
    unnamed x2, blocking collectives  649 us
    dot_general x16, matrix products, conv_backward(): jnp.einsum('ifd,cd->ifc', grad_padded[:, start:start + half], weight_tens...  46.2 us
    ppermute x16, starting transfers between devices, padded(): lax.ppermute(tail, axis, [(i, (i + 1) % count) for i in range(ends)])  43.2 us
    all_gather x1, blocking collectives, on_device(): lax.all_gather(device_shards[3], 'dp', axis=0, tiled=True)  35.6 us
    dot_general x16, matrix products, conv_forward(): jnp.einsum('ifc,cd->ifd', padded_frames[:, kernel_tap_index:kernel_tap_in...  30.7 us
    dot_general x24, matrix products, conv_backward(): jnp.einsum('ifc,ifd->cd', padded_frames[:, kernel_tap_index:kernel_tap_in...  29 us
    unnamed x368, local copies, waits for them, and re-layouts  28.6 us
    all_gather x1, waiting for transfers between devices, on_device(): lax.all_gather(device_shards[0], 'dp', axis=0, tiled=True)  26.5 us
  transfers between devices with their start and end apart: 41, of which 6 were waited for; matrix products, arithmetic and copies ran while one was open for 17% of the time, Pallas kernels for 0%

commit v1 on v0

v1 whole, which is shorter than its diff:
```python
import functools

import jax
import jax.numpy as jnp
from jax import lax
from jax.experimental import pallas as pl
from jax.experimental.pallas import tpu as pltpu
from jax.sharding import PartitionSpec as P

D = 512
S = 128
KERN = 3
LAYERS = 2
CONVS = 2 * LAYERS
PH = 128
STEP = 10
FRAMES = 1024
SEG = 16
RUN = FRAMES // SEG
HALF = D // 2
ITEMS = 2
PADDED = FRAMES + 2 * SEG
TABLE_ROWS = ITEMS * PH

NORM_EPS = 1e-05
HALF_ROOT = 0.7071067811865476
MOMENT_DECAY = 0.9
SQUARE_DECAY = 0.999
LEARN_RATE = 0.05
WEIGHT_DECAY = 0.01
ADAM_EPS = 1e-08

BF = jnp.bfloat16
F32 = jnp.float32
MESH = pl.DeviceIdType.MESH
HIGH = lax.Precision.HIGHEST

C_SCALE, C_SHIFT, C_INV, C_MI, C_ONE, C_2, C_3 = range(7)


def factor(ndp):
    return {16: (4, 2, 2), 128: (4, 8, 4)}.get(ndp, (4, ndp // 4, 1))


def dot(a, b):
    return jnp.dot(a, b, preferred_element_type=F32)


def dot_nt(a, b, precision=None):
    return lax.dot_general(a, b, (((1,), (1,)), ((), ())), preferred_element_type=F32, precision=precision)


def dot_tn(a, b, precision=None):
    return lax.dot_general(a, b, (((0,), (0,)), ((), ())), preferred_element_type=F32, precision=precision)


def fold(tile):
    rows, cols = tile.shape
    return jnp.sum(tile.reshape(rows // 8, 8, cols), axis=0)


def valid_rows(start, rows, count, value):
    i = lax.broadcasted_iota(jnp.int32, (rows, 128), 0)
    frame = (i & (SEG - 1)) * RUN + (i >> 4) + start // SEG
    return jnp.where(frame < count, jnp.float32(value), jnp.float32(0.0))


def train_kernel(cfg, *refs):
    ndp, (n0, n1, n2), slots = cfg["ndp"], cfg["dims"], cfg["slots"]
    shard, srows, remote_phon = cfg["shard"], cfg["srows"], cfg["remote_phon"]
    comm = cfg.get("comm", True)
    skip = cfg.get("skip", ())
    nq = ndp // CONVS
    nb = ndp // 8
    nz = cfg["chunks"]
    (
        phon, sv, fphone, cnt, cot, wmas, smas, brow, orow,
        o_frames, o_phone, o_small, o_gconv, o_gstyle,
        W, PAD, AT, ST, G, GY, COT, PM, OHP, TABLE, FPH, WM, SM, AE,
        SVR, PARS, PARR, COEF, STAT, BIAS, BGRAD, GSTS, GSTR, SX,
        DW, SIBR, RB, RA, ZR, GF, PGX,
        loc, ss, rs, s_z, r_z, s_f, r_f, s_s, r_s, s_b, r_b,
        rss, rsr, rbs, rbr, ras, rar, zs, zr,
    ) = refs
    SGS, SGR = PARS, PARR
    me = lax.axis_index("dp")
    c = lax.axis_index("seq")
    c0, c1, c2 = me // (n1 * n2), (me // n2) % n1, me % n2
    sib = (me, 1 - c)

    def remote(src, dst, send, recv, target):
        return pltpu.make_async_remote_copy(
            src_ref=src, dst_ref=dst, send_sem=send, recv_sem=recv, device_id=target, device_id_type=MESH
        )

    def wait_bytes(ref, sem):
        pltpu.make_async_copy(ref, ref, sem).wait()

    def sent(copy):
        copy.wait_send()

    def peers(fn):
        def one(d, carry):
            fn(lax.rem(me + d, ndp))
            return carry
        lax.fori_loop(1, ndp, one, 0)

    barrier = pltpu.get_barrier_semaphore()
    peers(lambda d: pl.semaphore_signal(barrier, inc=1, device_id=(d, c), device_id_type=MESH))
    pl.semaphore_signal(barrier, inc=1, device_id=sib, device_id_type=MESH)

    own_in = [
        pltpu.make_async_copy(wmas, WM, loc.at[0]),
        pltpu.make_async_copy(smas, SM, loc.at[1]),
        pltpu.make_async_copy(cot.at[c], COT.at[:, pl.ds(pl.multiple_of(c * HALF * 2, 512), 512)], loc.at[2]),
        pltpu.make_async_copy(fphone.at[c], FPH.at[:, pl.ds(pl.multiple_of(c * HALF * 2, 512), 512)], loc.at[3]),
    ]
    if remote_phon:
        own_in.append(
            pltpu.make_async_copy(
                phon.at[c, pl.ds(pl.multiple_of(me * 16, 16), 16)],
                TABLE.at[pl.ds(pl.multiple_of(me * 16, 16), 16)], loc.at[4],
            )
        )
    else:
        own_in.append(pltpu.make_async_copy(phon, TABLE, loc.at[4]))
    for copy in own_in:
        copy.start()

    own_in[0].wait()
    for cb in range(4):
        W[cb // 2, c0, c1, c2, :, (cb % 2) * 128:(cb % 2) * 128 + 128] = WM[
            pl.ds(cb, shard, stride=4), :
        ].astype(BF)
    own_in[1].wait()
    quarter = lax.rem(me, S // srows)
    for cb in range(8):
        block = SM[pl.ds(cb, srows, stride=8), :].astype(BF).astype(F32)
        for qq in range(S // srows):
            AE[qq * srows:(qq + 1) * srows, cb * 128:cb * 128 + 128] = jnp.where(quarter == qq, block, 0.0)
    vec = sv[c].astype(F32)
    vec = jnp.concatenate([jnp.broadcast_to(vec[i:i + 1], (4, S)) for i in range(ITEMS)], axis=0)
    SVR[me] = vec

    pl.semaphore_wait(barrier, ndp)

    def send_sv(d):
        return remote(SVR.at[me], SVR.at[me], ss.at[0], rs.at[0], (d, c))

    def send_phon(d):
        return remote(
            phon.at[c, pl.ds(pl.multiple_of(d * 16, 16), 16)],
            TABLE.at[pl.ds(pl.multiple_of(me * 16, 16), 16)], ss.at[1], rs.at[1], (d, c),
        )

    send_fph = remote(
        fphone.at[1 - c], FPH.at[:, pl.ds(pl.multiple_of(c * 512, 512), 512)], ss.at[2], rs.at[2], sib
    )
    send_cot = remote(
        cot.at[1 - c], COT.at[:, pl.ds(pl.multiple_of(c * 512, 512), 512)], ss.at[3], rs.at[3], sib
    )
    peers(lambda d: send_sv(d).start())
    if remote_phon:
        peers(lambda d: send_phon(d).start())
    send_fph.start()
    send_cot.start()

    rows = shard // nz

    def order(t):
        if t == 0:
            return c0
        return jnp.where(t - 1 < c0, t - 1, t)

    def z_hop(zz, q, up):
        to = c0 + (1 if up else -1)
        target = ((to * n1 + c1) * n2 + c2, c)
        piece = W.at[c, zz, c1, c2, pl.ds(q * rows, rows)]
        return remote(piece, piece, s_z.at[zz, q, 0 if up else 1], r_z.at[zz, q], target)

    def z_sends(zz, q, fn):
        @pl.when(jnp.logical_and(zz <= c0, c0 < n0 - 1))
        def _():
            fn(z_hop(zz, q, True))

        @pl.when(jnp.logical_and(zz >= c0, c0 > 0))
        def _():
            fn(z_hop(zz, q, False))

    def own_z(up, fn):
        for q in range(nz):
            @pl.when(c0 < n0 - 1 if up else c0 > 0)
            def _():
                fn(z_hop(c0, q, up))

    def first_sends(zz, fn):
        piece = W.at[c, zz, c1, c2]

        @pl.when(c == 0)
        def _():
            for k in range(1, n2):
                to = lax.rem(c2 + k, n2)
                fn(remote(piece, piece, s_f.at[zz, k], r_f.at[zz, k], ((c0 * n1 + c1) * n2 + to, c)))

        @pl.when(c == 1)
        def _():
            for k in range(1, n1):
                to = lax.rem(c1 + k, n1)
                fn(remote(piece, piece, s_f.at[zz, k], r_f.at[zz, k], ((c0 * n1 + to) * n2 + c2, c)))

    def second_sends(zz, fn):
        @pl.when(c == 0)
        def _():
            line = W.at[0, zz, c1]
            for k in range(1, n1):
                to = lax.rem(c1 + k, n1)
                fn(remote(line, line, s_s.at[zz, k], r_s.at[zz, k], ((c0 * n1 + to) * n2 + c2, c)))

        @pl.when(c == 1)
        def _():
            line = W.at[1, zz, :, c2]
            for k in range(1, n2):
                to = lax.rem(c2 + k, n2)
                fn(remote(line, line, s_s.at[zz, k], r_s.at[zz, k], ((c0 * n1 + c1) * n2 + to, c)))

    def first_wait(zz):
        @pl.when(c == 0)
        def _():
            for k in range(1, n2):
                wait_bytes(W.at[c, zz, c1, c2], r_f.at[zz, k])

        @pl.when(c == 1)
        def _():
            for k in range(1, n1):
                wait_bytes(W.at[c, zz, c1, c2], r_f.at[zz, k])

    def second_wait(zz):
        @pl.when(c == 0)
        def _():
            for k in range(1, n1):
                wait_bytes(W.at[0, zz, c1], r_s.at[zz, k])

        @pl.when(c == 1)
        def _():
            for k in range(1, n2):
                wait_bytes(W.at[1, zz, :, c2], r_s.at[zz, k])

    def sib_send(zz):
        return remote(W.at[c, zz], W.at[c, zz], s_b.at[zz], r_b.at[zz], sib)

    def ev0(t):
        zz = order(t)
        if t > 0:
            for q in range(nz):
                wait_bytes(W.at[c, zz, c1, c2, pl.ds(q * rows, rows)], r_z.at[zz, q])
                z_sends(zz, q, lambda copy: copy.start())

            @pl.when(zz == c0 - 1)
            def _():
                own_z(True, lambda copy: copy.start())
        first_sends(zz, lambda copy: copy.start())

    def ev1(t):
        zz = order(t)
        first_wait(zz)
        second_sends(zz, lambda copy: copy.start())

    def ev2(t):
        zz = order(t)
        second_wait(zz)
        sib_send(zz).start()

    def ev3(t):
        zz = order(t)
        wait_bytes(W.at[c, zz], r_b.at[zz])

    own_z(False, lambda copy: copy.start())

    @pl.when(c0 == 0)
    def _():
        own_z(True, lambda copy: copy.start())
    ev0(0)

    def make_perm(t, carry):
        r0 = pl.multiple_of(t * 128, 128)
        row = lax.broadcasted_iota(jnp.int32, (128, FRAMES), 0)
        col = lax.broadcasted_iota(jnp.int32, (128, FRAMES), 1)
        frame = (row & (SEG - 1)) * RUN + (row >> 4) + r0 // SEG
        PM[pl.ds(r0, 128), :] = jnp.where(col == frame, 1.0, 0.0).astype(BF)
        return carry

    lax.fori_loop(0, FRAMES // 128, make_perm, 0)

    row_kind = lax.broadcasted_iota(jnp.int32, (ndp * 8, 1), 0) & 3
    wait_bytes(SVR.at[pl.ds(0, ndp - 1)], rs.at[0])
    svall = SVR[...].reshape(ndp * 8, S)
    acc = jnp.zeros((ndp * 8, 256), F32)
    for b in range(4):
        acc = acc + dot(
            jnp.where(row_kind == b, svall, 0.0).astype(BF), AE[:, b * 256:b * 256 + 256].astype(BF)
        )
    offset_kind = lax.rem(me, nq) * 4 // nq
    acc = acc + jnp.where(row_kind == offset_kind, orow[0:1, :].astype(BF).astype(F32), 0.0)
    PARS[:, :, 0:256] = acc.reshape(ndp, 8, 256)
    PARS[:, :, 256:384] = jnp.broadcast_to(brow[0:1, :].astype(BF).astype(F32).reshape(1, 1, 128), (ndp, 8, 128))

    def send_par(d):
        return remote(PARS.at[d], PARR.at[me], ss.at[4], rs.at[4], (d, c))

    peers(lambda d: send_par(d).start())
    PARR[me] = PARS[me]

    own_in[3].wait()
    wait_bytes(FPH.at[:, pl.ds(0, 512)], rs.at[2])
    for i in range(ITEMS):
        phone = FPH[i:i + 1, :]
        if slots & (slots - 1) == 0:
            shift = slots.bit_length() - 1
            place = ((phone >> shift) << (shift + 1)) + i * slots + (phone & (slots - 1))
        else:
            place = (phone // slots) * (2 * slots) + i * slots + phone % slots
        slot = lax.broadcasted_iota(jnp.int32, (TABLE_ROWS, FRAMES), 0)
        onehot = jnp.where(slot == place, 1.0, 0.0).astype(BF)
        for t in range(4):
            OHP[i, :, t * 256:t * 256 + 256] = dot_nt(onehot, PM[t * 256:t * 256 + 256, :]).astype(BF)

    STAT[...] = jnp.zeros(STAT.shape, F32)
    own_in[4].wait()
    if remote_phon:
        wait_bytes(TABLE.at[pl.ds(0, 16 * (ndp - 1))], rs.at[1])
    for i in range(ITEMS):
        count = cnt[c, i]
        for t in range(4):
            x = dot(OHP[i, :, t * 256:t * 256 + 256].T, TABLE[...])
            mask = valid_rows(t * 256, 256, count, 1.0)
            x = x * jnp.concatenate([mask] * 4, axis=1)
            ST[0, i, t * 256:t * 256 + 256, :] = x.astype(BF)
            STAT[i, 0] += fold(x)
            STAT[i, 1] += fold(x * x)

    ev1(0)
    own_in[2].wait()
    wait_bytes(COT.at[:, pl.ds(0, 512)], rs.at[3])
    for i in range(ITEMS):
        count = cnt[c, i]

        def permute(t, carry):
            r0 = pl.multiple_of(t * 256, 256)
            y = dot(PM[pl.ds(r0, 256), :], COT[i])
            mask = valid_rows(r0, 256, count, 1.0)
            G[i, pl.ds(r0, 256), :] = (y * jnp.concatenate([mask] * 4, axis=1)).astype(BF)
            return carry

        lax.fori_loop(0, 4, permute, 0)

    wait_bytes(PARR.at[pl.ds(0, ndp - 1)], rs.at[4])
    for j in range(CONVS):
        total = jnp.sum(PARR[j * nq:(j + 1) * nq, :, 0:256], axis=0)
        for i in range(ITEMS):
            for b in range(4):
                COEF[j, i, 8 + b // 2:9 + b // 2, (b % 2) * 256:(b % 2) * 256 + 256] = total[
                    4 * i + b:4 * i + b + 1, :
                ]
    for l in range(LAYERS):
        for qb in range(4):
            first = l * (ndp // 2) + qb * nb
            BIAS[l, :, qb * 128:qb * 128 + 128] = jnp.sum(PARR[first:first + nb, :, 256:384], axis=0)

    def stats_to_coef(j):
        for i in range(ITEMS):
            n = cnt[c, i].astype(F32)
            sums = jnp.sum(STAT[i, 0], axis=0, keepdims=True)
            squares = jnp.sum(STAT[i, 1], axis=0, keepdims=True)
            mean = sums / n
            var = jnp.maximum(squares / n - mean * mean, 0.0)
            inv = lax.rsqrt(var + NORM_EPS)
            one = (1.0 + COEF[j, i, 8:9]) * inv
            shift = COEF[j, i, 9:10] - mean * one

            def put(k, v):
                COEF[j, i, k:k + 1] = v
            put(C_SCALE, 0.5 * one)
            put(C_SHIFT, 0.5 * shift)
            put(C_INV, inv)
            put(C_MI, mean * inv)
            put(C_ONE, one)

    def coef(j, i, k, cols):
        return COEF[j, i, k:k + 1, cols]

    def edges():
        row = lax.broadcasted_iota(jnp.int32, (SEG, D), 0)
        for i in range(ITEMS):
            last = PAD[i, FRAMES:FRAMES + SEG, :].astype(F32)
            head = jnp.where(row == 0, 0.0, pltpu.roll(last, 1, 0))
            PAD[i, 0:SEG, :] = head.astype(BF)
            first = PAD[i, SEG:2 * SEG, :].astype(F32)
            tail = jnp.where(row == SEG - 1, 0.0, pltpu.roll(first, SEG - 1, 0))
            PAD[i, FRAMES + SEG:PADDED, :] = tail.astype(BF)

    TR = 128

    def adain_forward(j):
        stats_to_coef(j)
        for i in range(ITEMS):
            count = cnt[c, i]

            def tile(t, carry):
                r0 = pl.multiple_of(t * TR, TR)
                mask = valid_rows(r0, TR, count, 1.0)
                for cb in range(4):
                    cols = slice(cb * 128, cb * 128 + 128)
                    x = ST[j, i, pl.ds(r0, TR), cols].astype(F32)
                    v = x * coef(j, i, C_SCALE, cols) + coef(j, i, C_SHIFT, cols)
                    a = ((v + v * jnp.tanh(v)) * mask).astype(BF)
                    PAD[i, pl.ds(r0 + SEG, TR), cols] = a
                    AT[j, cols, pl.ds(i * FRAMES + r0, TR)] = a.T
                return carry

            lax.fori_loop(0, FRAMES // TR, tile, 0)
        edges()

    M = 512

    def taps(j):
        return [W[h, j].reshape(KERN * D, HALF) for h in range(2)]

    def conv_forward(j, epilogue):
        def tile(t, carry):
            i = t // (FRAMES // M)
            r0 = pl.multiple_of(lax.rem(t, FRAMES // M) * M, M)
            for h in range(2):
                acc = None
                weights = W[h, j].reshape(KERN * D, HALF)
                for k in range(KERN):
                    part = dot(PAD[i, pl.ds(r0 + SEG * k, M), :], weights[k * D:(k + 1) * D])
                    acc = part if acc is None else acc + part
                epilogue(i, r0, h, acc)
            return carry
        lax.fori_loop(0, ITEMS * FRAMES // M, tile, 0)

    def middle_out(j):
        def epilogue(i, r0, h, acc):
            count = cnt[c, i]
            for rb in range(0, M, 128):
                mask = valid_rows(r0 + rb, 128, count, 1.0)
                for cb in range(2):
                    cols = slice(h * HALF + cb * 128, h * HALF + cb * 128 + 128)
                    p = acc[rb:rb + 128, cb * 128:cb * 128 + 128]
                    ST[j + 1, i, pl.ds(r0 + rb, 128), cols] = p.astype(BF)
                    kept = p * mask
                    STAT[i, 0, :, cols] += fold(kept)
                    STAT[i, 1, :, cols] += fold(kept * p)
        return epilogue

    def block_out(l):
        def epilogue(i, r0, h, acc):
            count = cnt[c, i]
            for rb in range(0, M, 128):
                mask = valid_rows(r0 + rb, 128, count, HALF_ROOT)
                for cb in range(2):
                    cols = slice(h * HALF + cb * 128, h * HALF + cb * 128 + 128)
                    q = acc[rb:rb + 128, cb * 128:cb * 128 + 128] + BIAS[l, 0:1, cols]
                    x = (ST[2 * l, i, pl.ds(r0 + rb, 128), cols].astype(F32) + q) * mask
                    if l < LAYERS - 1:
                        ST[2 * l + 2, i, pl.ds(r0 + rb, 128), cols] = x.astype(BF)
                        STAT[i, 0, :, cols] += fold(x)
                        STAT[i, 1, :, cols] += fold(x * x)
                    else:
                        COT[i, pl.ds(r0 + rb, 128), cols] = x.astype(BF)
        return epilogue

    adain_forward(0)
    STAT[...] = jnp.zeros(STAT.shape, F32)
    ev0(1)
    ev2(0)
    ev1(1)
    ev0(2)
    ev2(1)
    ev1(2)
    ev3(0)
    ev3(1)
    conv_forward(0, middle_out(0))
    ev0(3)
    adain_forward(1)
    STAT[...] = jnp.zeros(STAT.shape, F32)
    ev2(2)
    ev1(3)
    ev3(2)
    conv_forward(1, block_out(0))
    adain_forward(2)
    STAT[...] = jnp.zeros(STAT.shape, F32)
    ev2(3)
    ev3(3)
    conv_forward(2, middle_out(2))
    adain_forward(3)
    conv_forward(3, block_out(1))

    def weight_grad(j):
        MW = 256

        def tile(t, carry):
            r0 = pl.multiple_of(t * MW, MW)
            for k in range(KERN):
                for h in range(2):
                    acc = None
                    for i in range(ITEMS):
                        part = dot(
                            AT[j, pl.ds(r0, MW), i * FRAMES:(i + 1) * FRAMES],
                            PAD[i, (2 - k) * SEG:(2 - k) * SEG + FRAMES, h * HALF:(h + 1) * HALF],
                        )
                        acc = part if acc is None else acc + part
                    DWF.at[j, h][pl.ds(k * D + r0, MW), :] = acc.astype(BF)
            return carry

        lax.fori_loop(0, D // MW, tile, 0)

    DWF = DW.reshape(CONVS, 2, KERN * D, HALF)

    def input_grad(j):
        STAT[...] = jnp.zeros(STAT.shape, F32)

        def tile(t, carry):
            i = t // (FRAMES // M)
            r0 = pl.multiple_of(lax.rem(t, FRAMES // M) * M, M)
            count = cnt[c, i]
            for n in range(2):
                acc = None
                for k in range(KERN):
                    for h in range(2):
                        weights = W[h, j].reshape(KERN * D, HALF)
                        part = dot_nt(
                            PAD[i, pl.ds(r0 + SEG * (2 - k), M), h * HALF:(h + 1) * HALF],
                            weights[k * D + n * HALF:k * D + (n + 1) * HALF],
                        )
                        acc = part if acc is None else acc + part
                for rb in range(0, M, 128):
                    mask = valid_rows(r0 + rb, 128, count, 0.5)
                    for cb in range(2):
                        cols = slice(n * HALF + cb * 128, n * HALF + cb * 128 + 128)
                        x = ST[j, i, pl.ds(r0 + rb, 128), cols].astype(F32)

                        def cf(k):
                            return COEF[j, i, k:k + 1, cols]
                        v = x * cf(C_SCALE) + cf(C_SHIFT)
                        th = jnp.tanh(v)
                        u = acc[rb:rb + 128, cb * 128:cb * 128 + 128] * mask
                        gy = (u + u * th) * (1.0 + v * (1.0 - th))
                        xhat = x * cf(C_INV) - cf(C_MI)
                        STAT[i, 0, :, cols] += fold(gy)
                        STAT[i, 1, :, cols] += fold(gy * xhat)
                        GY[i, pl.ds(r0 + rb, 128), cols] = gy.astype(BF)
            return carry

        lax.fori_loop(0, ITEMS * FRAMES // M, tile, 0)

    def send_gst(j, fn):
        def one(q, carry):
            d = j * nq + q
            variant = lax.rem(lax.rem(d, ndp // 2) // nb, 2)

            @pl.when(d != me)
            def _():
                fn(remote(GSTS.at[j, variant], GSTR.at[me], ss.at[5], rs.at[5], (d, c)))
            return carry
        lax.fori_loop(0, nq, one, 0)

    def adain_sums(j):
        for i in range(ITEMS):
            n = cnt[c, i].astype(F32)
            gt = jnp.sum(STAT[i, 0], axis=0, keepdims=True)
            gs = jnp.sum(STAT[i, 1], axis=0, keepdims=True)
            one, inv, mi = (COEF[j, i, k:k + 1] for k in (C_ONE, C_INV, C_MI))
            each = one / n
            COEF[j, i, C_2:C_2 + 1] = each * (gt - mi * gs)
            COEF[j, i, C_3:C_3 + 1] = each * inv * gs
            for b in range(4):
                part = (gs if b < 2 else gt)[:, (b % 2) * 256:(b % 2) * 256 + 256]
                for v in range(2):
                    GSTS[j, v, 4 * i + b:4 * i + b + 1, 0:256] = part
        for v in range(2):
            qb = (j % 2) * 2 + v
            GSTS[j, v, :, 256:384] = jnp.broadcast_to(
                BGRAD[j // 2, 0:1, qb * 128:qb * 128 + 128], (8, 128)
            )
        variant_me = lax.rem(lax.rem(me, ndp // 2) // nb, 2)

        @pl.when(me // nq == j)
        def _():
            GSTR[me] = GSTS[j, variant_me]
        send_gst(j, lambda copy: copy.start())

    def adain_backward(j):
        adain_sums(j)
        for i in range(ITEMS):
            count = cnt[c, i]

            def tile(t, carry):
                r0 = pl.multiple_of(t * TR, TR)
                mask = valid_rows(r0, TR, count, 1.0)
                for cb in range(4):
                    cols = slice(cb * 128, cb * 128 + 128)
                    gy = GY[i, pl.ds(r0, TR), cols].astype(F32)
                    x = ST[j, i, pl.ds(r0, TR), cols].astype(F32)
                    gh = gy * coef(j, i, C_ONE, cols) - x * coef(j, i, C_3, cols) - coef(j, i, C_2, cols)
                    gh = gh * mask
                    if j % 2 == 1:
                        PAD[i, pl.ds(r0 + SEG, TR), cols] = gh.astype(BF)
                    else:
                        g = G[i, pl.ds(r0, TR), cols].astype(F32) * HALF_ROOT + gh
                        if j > 0:
                            G[i, pl.ds(r0, TR), cols] = g.astype(BF)
                            g = g * HALF_ROOT
                            BGRAD[j // 2 - 1, :, cols] += fold(g.astype(BF).astype(F32))
                        PAD[i, pl.ds(r0 + SEG, TR), cols] = g.astype(BF)
                return carry

            lax.fori_loop(0, FRAMES // TR, tile, 0)
        if j > 0:
            edges()
        if j > 0 and j % 2 == 0:
            close_bias(j // 2 - 1)

    def close_bias(l):
        BGRAD[l] = jnp.broadcast_to(jnp.sum(BGRAD[l], axis=0, keepdims=True), (8, D))

    def rs_sib(j):
        return remote(DW.at[j, 1 - c], SIBR.at[j], rss.at[j], rsr.at[j], sib)

    def rs_second(j, fn):
        @pl.when(c == 0)
        def _():
            for k in range(1, n1):
                to = lax.rem(c1 + k, n1)
                fn(remote(DW.at[j, 0, to], RB.at[j, pl.ds((k - 1) * n2, n2)], rbs.at[j, k], rbr.at[j, k],
                          ((c0 * n1 + to) * n2 + c2, c)))

        @pl.when(c == 1)
        def _():
            for k in range(1, n2):
                to = lax.rem(c2 + k, n2)
                fn(remote(DW.at[j, 1, :, to], RB.at[j, pl.ds((k - 1) * n1, n1)], rbs.at[j, k], rbr.at[j, k],
                          ((c0 * n1 + c1) * n2 + to, c)))

    def rs_first(j, fn):
        @pl.when(c == 0)
        def _():
            for k in range(1, n2):
                to = lax.rem(c2 + k, n2)
                fn(remote(DW.at[j, 0, c1, to], RA.at[j, k - 1], ras.at[j, k], rar.at[j, k],
                          ((c0 * n1 + c1) * n2 + to, c)))

        @pl.when(c == 1)
        def _():
            for k in range(1, n1):
                to = lax.rem(c1 + k, n1)
                fn(remote(DW.at[j, 1, to, c2], RA.at[j, k - 1], ras.at[j, k], rar.at[j, k],
                          ((c0 * n1 + to) * n2 + c2, c)))

    def rs_plane(j, fn):
        @pl.when(c0 != j)
        def _():
            k = lax.rem(c0 - j + n0, n0)
            fn(remote(DW.at[j, c, c1, c2], ZR.at[k - 1], zs.at[j], zr.at[k], ((j * n1 + c1) * n2 + c2, c)))

    def rv0(j):
        rs_sib(j).start()

    def rv1(j):
        wait_bytes(SIBR.at[j], rsr.at[j])

        def one(y, carry):
            for x in range(n2):
                DW[j, c, y, x] = (DW[j, c, y, x].astype(F32) + SIBR[j, y, x].astype(F32)).astype(BF)
            return carry
        lax.fori_loop(0, n1, one, 0)
        rs_second(j, lambda copy: copy.start())

    def rv2(j):
        @pl.when(c == 0)
        def _():
            for k in range(1, n1):
                wait_bytes(RB.at[j, pl.ds((k - 1) * n2, n2)], rbr.at[j, k])
            for x in range(n2):
                total = DW[j, 0, c1, x].astype(F32)
                for k in range(1, n1):
                    total = total + RB[j, (k - 1) * n2 + x].astype(F32)
                DW[j, 0, c1, x] = total.astype(BF)

        @pl.when(c == 1)
        def _():
            for k in range(1, n2):
                wait_bytes(RB.at[j, pl.ds((k - 1) * n1, n1)], rbr.at[j, k])
            for y in range(n1):
                total = DW[j, 1, y, c2].astype(F32)
                for k in range(1, n2):
                    total = total + RB[j, (k - 1) * n1 + y].astype(F32)
                DW[j, 1, y, c2] = total.astype(BF)
        rs_first(j, lambda copy: copy.start())

    def rv3(j):
        def add(n):
            for k in range(1, n):
                wait_bytes(RA.at[j, k - 1], rar.at[j, k])
            total = DW[j, c, c1, c2].astype(F32)
            for k in range(1, n):
                total = total + RA[j, k - 1].astype(F32)
            DW[j, c, c1, c2] = total.astype(BF)

        @pl.when(c == 0)
        def _():
            add(n2)

        @pl.when(c == 1)
        def _():
            add(n1)
        rs_plane(j, lambda copy: copy.start())

    BGRAD[...] = jnp.zeros(BGRAD.shape, F32)
    for i in range(ITEMS):
        def enter(t, carry):
            r0 = pl.multiple_of(t * TR, TR)
            g = (G[i, pl.ds(r0, TR), :].astype(F32) * HALF_ROOT).astype(BF)
            PAD[i, pl.ds(r0 + SEG, TR), :] = g
            BGRAD[LAYERS - 1] += fold(g.astype(F32))
            return carry
        lax.fori_loop(0, FRAMES // TR, enter, 0)
    edges()
    close_bias(LAYERS - 1)

    weight_grad(3)
    rv0(3)
    input_grad(3)
    rv1(3)
    adain_backward(3)
    weight_grad(2)
    rv0(2)
    rv2(3)
    input_grad(2)
    rv3(3)
    rv1(2)
    adain_backward(2)
    weight_grad(1)
    rv0(1)
    rv2(2)
    input_grad(1)
    rv3(2)
    rv1(1)
    adain_backward(1)
    weight_grad(0)
    rv0(0)
    rv2(1)
    input_grad(0)
    rv3(1)
    rv1(0)
    adain_backward(0)

    for n in range(2):
        cols = slice(n * HALF, (n + 1) * HALF)
        pg = dot(OHP[0], PAD[0, SEG:SEG + FRAMES, cols]) + dot(OHP[1], PAD[1, SEG:SEG + FRAMES, cols])

        @pl.when(c == n)
        def _():
            PGX[c] = pg.astype(BF)

        @pl.when(c != n)
        def _():
            TABLE[:, 0:HALF] = pg.astype(BF)
    send_pgx = remote(TABLE.at[:, pl.ds(0, HALF)], PGX.at[c], ss.at[6], rs.at[6], sib)
    send_pgx.start()
    rv2(0)

    def unpermute(t, carry):
        f0 = pl.multiple_of(t * 256, 256)
        back = PM[:, pl.ds(f0, 256)].T
        for i in range(ITEMS):
            GY[i, pl.ds(f0, 256), :] = dot(back, COT[i]).astype(BF)
        return carry

    lax.fori_loop(0, FRAMES // 256, unpermute, 0)
    send_frames = remote(
        GY.at[:, pl.ds(pl.multiple_of((1 - c) * 512, 512), 512)], o_frames.at[c], ss.at[7], rs.at[7], sib
    )
    send_frames.start()
    keep_frames = pltpu.make_async_copy(
        GY.at[:, pl.ds(pl.multiple_of(c * 512, 512), 512)], o_frames.at[c], loc.at[5]
    )
    keep_frames.start()

    wait_bytes(PGX.at[0], rs.at[6])

    def send_pg(d):
        return remote(
            PGX.at[:, pl.ds(pl.multiple_of(d * 16, 16), 16)],
            o_phone.at[:, pl.ds(pl.multiple_of(me * 16, 16), 16)], ss.at[8], rs.at[8], (d, c),
        )

    if remote_phon:
        peers(lambda d: send_pg(d).start())
        mine = pl.ds(pl.multiple_of(me * 16, 16), 16)
        o_phone[:, mine] = PGX[:, mine]
    else:
        o_phone[...] = PGX[...]

    wait_bytes(GSTR.at[pl.ds(0, ndp - 1)], rs.at[5])
    gall = GSTR[:, :, 0:256].reshape(ndp * 8, 256)
    back_rows = jnp.zeros((ndp * 8, S), F32)
    for b in range(4):
        picked = jnp.where(row_kind == b, svall_of(SVR, ndp), 0.0)
        da = dot_tn(picked, gall, HIGH)
        part = None
        for qq in range(S // srows):
            piece = jnp.where(quarter == qq, da[qq * srows:(qq + 1) * srows], 0.0)
            part = piece if part is None else part + piece
        SX[0, 0:srows, b * 256:b * 256 + 256] = part
        back_rows = back_rows + dot_nt(
            jnp.where(row_kind == b, gall, 0.0), AE[:, b * 256:b * 256 + 256], HIGH
        )
    peers(lambda d: sent(send_par(d)))
    SGS[:, :, 0:S] = back_rows.reshape(ndp, 8, S)

    def send_sg(d):
        return remote(SGS.at[d, :, pl.ds(0, S)], SGR.at[me, :, pl.ds(0, S)], ss.at[9], rs.at[9], (d, c))

    peers(lambda d: send_sg(d).start())
    SGR[me, :, 0:S] = SGS[me, :, 0:S]
    SX[0, srows:srows + 8, :] = jnp.zeros((8, 1024), F32)
    SX[0, srows:srows + 1, 0:256] = jnp.sum(jnp.where(row_kind == offset_kind, gall, 0.0), axis=0, keepdims=True)
    SX[0, srows:srows + 1, 256:384] = jnp.sum(GSTR[:, 0:1, 256:384], axis=0)
    rv3(0)
    wait_bytes(SGR.at[pl.ds(0, ndp - 1), :, pl.ds(0, S)], rs.at[9])
    sg = jnp.sum(SGR[:, :, 0:S], axis=0)
    for i in range(ITEMS):
        SX[0, srows + 1 + i:srows + 2 + i, 0:S] = jnp.sum(sg[4 * i:4 * i + 4], axis=0, keepdims=True)
    send_sx = remote(SX.at[0], SX.at[1], ss.at[10], rs.at[10], sib)
    send_sx.start()

    total = DW[c0, c, c1, c2].astype(F32)
    for k in range(1, n0):
        wait_bytes(ZR.at[k - 1], zr.at[k])
        total = total + ZR[k - 1].astype(F32)
    GF[c] = total
    send_gf = remote(GF.at[c], GF.at[c], ss.at[11], rs.at[11], sib)
    send_gf.start()

    wait_bytes(SX.at[1], rs.at[10])
    o_small[0] = SX[0, srows:srows + 8, 0:384] + SX[1, srows:srows + 8, 0:384]
    o_small[1 + c] = SX[0, srows:srows + 8, 0:384]
    o_small[2 - c] = SX[1, srows:srows + 8, 0:384]
    for cb in range(8):
        cols = slice(cb * 128, cb * 128 + 128)
        o_gstyle[pl.ds(cb, srows, stride=8), :] = SX[0, 0:srows, cols] + SX[1, 0:srows, cols]
    wait_bytes(GF.at[c], rs.at[11])
    for cb in range(4):
        o_gconv[pl.ds(cb, shard, stride=4), :] = GF[cb // 2, :, (cb % 2) * 128:(cb % 2) * 128 + 128]

    if remote_phon:
        wait_bytes(o_phone.at[:, pl.ds(0, 16 * (ndp - 1))], rs.at[8])
    wait_bytes(GY.at[:, pl.ds(0, 512)], rs.at[7])
    keep_frames.wait()

    peers(lambda d: sent(send_sv(d)))
    if remote_phon:
        peers(lambda d: sent(send_phon(d)))
        peers(lambda d: sent(send_pg(d)))
    peers(lambda d: sent(send_sg(d)))
    for copy in (send_fph, send_cot, send_pgx, send_frames, send_sx, send_gf):
        sent(copy)
    for j in range(CONVS):
        send_gst(j, sent)
        sent(rs_sib(j))
        rs_second(j, sent)
        rs_first(j, sent)
        rs_plane(j, sent)
    own_z(False, sent)
    own_z(True, sent)
    for t in range(n0):
        zz = order(t)
        if t > 0:
            for q in range(nz):
                z_sends(zz, q, sent)
        first_sends(zz, sent)
        second_sends(zz, sent)
        sent(sib_send(zz))


def svall_of(SVR, ndp):
    return SVR[...].reshape(ndp * 8, S)


def run_train(cfg, phon, sv, fphone, cnt, cot, wmas, smas, brow, orow):
    ndp, (n0, n1, n2) = cfg["ndp"], cfg["dims"]
    shard, srows = cfg["shard"], cfg["srows"]
    nz = cfg["chunks"]
    nmax = max(n1, n2)
    vm = pltpu.VMEM
    dma = pltpu.SemaphoreType.DMA
    any_ = pl.BlockSpec(memory_space=pl.ANY)
    vmem = pl.BlockSpec(memory_space=pltpu.VMEM)
    smem = pl.BlockSpec(memory_space=pltpu.SMEM)
    scratch = [
        vm((2, n0, n1, n2, shard, HALF), BF),
        vm((ITEMS, PADDED, D), BF),
        vm((CONVS, D, ITEMS * FRAMES), BF),
        vm((CONVS, ITEMS, FRAMES, D), BF),
        vm((ITEMS, FRAMES, D), BF),
        vm((ITEMS, FRAMES, D), BF),
        vm((ITEMS, FRAMES, D), BF),
        vm((FRAMES, FRAMES), BF),
        vm((ITEMS, TABLE_ROWS, FRAMES), BF),
        vm((TABLE_ROWS, D), BF),
        vm((ITEMS, FRAMES), jnp.int32),
        vm((shard * 4, 128), F32),
        vm((srows * 8, 128), F32),
        vm((S, 1024), F32),
        vm((ndp, 8, S), F32),
        vm((ndp, 8, 384), F32),
        vm((ndp, 8, 384), F32),
        vm((CONVS, ITEMS, 16, D), F32),
        vm((ITEMS, 2, 8, D), F32),
        vm((LAYERS, 8, D), F32),
        vm((LAYERS, 8, D), F32),
        vm((CONVS, 2, 8, 384), F32),
        vm((ndp, 8, 384), F32),
        vm((2, srows + 8, 1024), F32),
        vm((CONVS, 2, n1, n2, shard, HALF), BF),
        vm((CONVS, n1, n2, shard, HALF), BF),
        vm((CONVS, max((n1 - 1) * n2, (n2 - 1) * n1), shard, HALF), BF),
        vm((CONVS, nmax - 1, shard, HALF), BF),
        vm((n0 - 1, shard, HALF), BF),
        vm((2, shard, HALF), F32),
        vm((2, TABLE_ROWS, HALF), BF),
        dma((6,)), dma((12,)), dma((12,)),
        dma((n0, nz, 2)), dma((n0, nz)),
        dma((n0, nmax)), dma((n0, nmax)),
        dma((n0, nmax)), dma((n0, nmax)),
        dma((n0,)), dma((n0,)),
        dma((CONVS,)), dma((CONVS,)),
        dma((CONVS, nmax)), dma((CONVS, nmax)),
        dma((CONVS, nmax)), dma((CONVS, nmax)),
        dma((CONVS,)), dma((n0,)),
    ]
    return pl.pallas_call(
        functools.partial(train_kernel, cfg),
        out_shape=(
            jax.ShapeDtypeStruct((2, ITEMS, FRAMES // 2, D), BF),
            jax.ShapeDtypeStruct((2, TABLE_ROWS, HALF), BF),
            jax.ShapeDtypeStruct((3, 8, 384), F32),
            jax.ShapeDtypeStruct((shard * 4, 128), F32),
            jax.ShapeDtypeStruct((srows * 8, 128), F32),
        ),
        in_specs=[any_, vmem, any_, smem, any_, any_, any_, vmem, vmem],
        out_specs=(any_, vmem, vmem, vmem, vmem),
        scratch_shapes=scratch,
        compiler_params=pltpu.CompilerParams(
            collective_id=0, has_side_effects=True, vmem_limit_bytes=63 * 2**20
        ),
    )(phon, sv, fphone, cnt, cot, wmas, smas, brow, orow)


def adamw_update(master, moment, square, gradient, step_value):
    new_moment = MOMENT_DECAY * moment + (1.0 - MOMENT_DECAY) * gradient
    new_square = SQUARE_DECAY * square + (1.0 - SQUARE_DECAY) * gradient * gradient
    first_fix = 1.0 - jnp.power(jnp.float32(MOMENT_DECAY), step_value)
    second_fix = 1.0 - jnp.power(jnp.float32(SQUARE_DECAY), step_value)
    updated = master - LEARN_RATE * (
        new_moment / first_fix / (jnp.sqrt(new_square / second_fix) + ADAM_EPS)
        + WEIGHT_DECAY * master
    )
    return (updated, new_moment, new_square, updated.astype(BF))


def on_device(
    phonemes, style_vector, frame_phone, frame_count, cotangent,
    conv_master, conv_moment, conv_square, bias_master, bias_moment, bias_square,
    style_master, style_moment, style_square, offset_master, offset_moment, offset_square,
):
    ndp = lax.axis_size("dp")
    micros, items, slots, _ = phonemes.shape
    shard = conv_master.shape[0] // D
    srows = style_master.shape[0] // (2 * D)
    bsize, osize = bias_master.shape[0], offset_master.shape[0]
    remote_phon = (ITEMS * slots) % 16 == 0
    cfg = dict(
        ndp=ndp, dims=factor(ndp), slots=slots, shard=shard, srows=srows, remote_phon=remote_phon,
        chunks=2 if shard % 32 == 0 else 1,
    )
    me = lax.axis_index("dp")
    c = lax.axis_index("seq")
    if remote_phon:
        phon = phonemes.reshape(micros, items * slots, D)
    else:
        mine = lax.dynamic_index_in_dim(phonemes, c, 0, keepdims=False)
        mine = mine.reshape(ndp, ITEMS * slots, D)
        phon = lax.all_to_all(mine, "dp", split_axis=0, concat_axis=0, tiled=True).reshape(TABLE_ROWS, D)
    spread = 128 // bsize
    brow = jnp.where(
        jnp.arange(128) // bsize == me % spread, jnp.tile(bias_master, spread), 0.0
    ).reshape(1, 128)
    if osize == 256:
        orow = offset_master.reshape(1, 256)
    else:
        wide = 256 // osize
        orow = jnp.where(
            jnp.arange(256) // osize == me % wide, jnp.tile(offset_master, wide), 0.0
        ).reshape(1, 256)
    frames, phone, small, gconv, gstyle = run_train(
        cfg, phon, style_vector, frame_phone, frame_count, cotangent,
        conv_master.reshape(shard * 4, 128), style_master.reshape(srows * 8, 128), brow, orow,
    )
    if remote_phon:
        phone_grads = phone.reshape(micros, items, slots, HALF).astype(F32)
    else:
        moved = lax.all_to_all(
            phone.reshape(micros, ndp, ITEMS * slots, HALF), "dp", split_axis=1, concat_axis=1, tiled=True
        )
        phone_grads = moved.reshape(micros, items, slots, HALF).astype(F32)
    style_grads = small[1:3, 1:3, 0:S]
    gbias = lax.dynamic_slice(small[0, 0, 256:384], ((me % spread) * bsize,), (bsize,))
    goff = small[0, 0, 0:256]
    if osize != 256:
        goff = lax.dynamic_slice(goff, ((me % (256 // osize)) * osize,), (osize,))
    step_value = jnp.float32(STEP)
    conv_out = adamw_update(conv_master, conv_moment, conv_square, gconv.reshape(-1), step_value)
    bias_out = adamw_update(bias_master, bias_moment, bias_square, gbias, step_value)
    style_out = adamw_update(style_master, style_moment, style_square, gstyle.reshape(-1), step_value)
    offset_out = adamw_update(offset_master, offset_moment, offset_square, goff, step_value)
    return (
        frames.astype(F32), phone_grads, style_grads, *conv_out, *bias_out, *style_out, *offset_out,
    )


def solution(mesh):
    return jax.shard_map(
        on_device,
        mesh=mesh,
        in_specs=(
            P(None, None, "dp", None), P(None, "dp", None), P(None, "dp", "seq"), P(None, "dp"),
            P(None, "dp", "seq", None), *[P("dp")] * 12,
        ),
        out_specs=(
            P(None, "dp", "seq", None), P(None, None, "dp", "seq"), P(None, "dp", None), *[P("dp")] * 16,
        ),
        check_vma=False,
    )
```

time: 1170 us -> 177 us (0.15)
  blocking collectives: 717 us -> 0 us
  Pallas kernels: 0 us -> 162 us
  matrix products: 152 us -> 0 us
  starting transfers between devices: 90.5 us -> 0 us
  local copies, waits for them, and re-layouts: 64 us -> 3.48 us
  waiting for transfers between devices: 54.8 us -> 0 us
  other arithmetic: 63.8 us -> 9.62 us
  between operations: 20 us -> 0.82 us
    unnamed x2 -> x0, blocking collectives: 649 us -> none
    pallas_call x0 -> x1, Pallas kernels: none -> 162 us  [run_train(): pl.pallas_call(functools.partial(train_kernel, cfg), out_shape=(jax.Shape...]
    dot_general x100 -> x0, matrix products: 152 us -> none  [the longest x16 46.2 us: conv_backward(): jnp.einsum('ifd,cd->ifc', grad_padded[:, start:start + half], weight_tens...]
    ppermute x32 -> x0, starting transfers between devices: 64.8 us -> none  [the longest x16 43.2 us: padded(): lax.ppermute(tail, axis, [(i, (i + 1) % count) for i in range(ends)])]
    all_gather x1 -> x0, blocking collectives: 35.6 us -> none  [on_device(): lax.all_gather(device_shards[3], 'dp', axis=0, tiled=True)]
    psum x9 -> x0, blocking collectives: 32.6 us -> none  [the longest x4 15.7 us: adain_backward(): lax.psum((jnp.sum(grad_shaped, axis=1), jnp.sum(grad_shaped * normed, axi...]
    unnamed x368 -> x30, local copies, waits for them, and re-layouts: 28.6 us -> 0.09 us
    all_gather x2 -> x0, waiting for transfers between devices: 26.5 us -> none  [the longest x1 26.5 us: on_device(): lax.all_gather(device_shards[0], 'dp', axis=0, tiled=True)]
  transfers between devices with their start and end apart: 41 -> 0, of which waited for: 6 -> 0; matrix products, arithmetic and copies ran while one was open for 17% -> 0% of each run, Pallas kernels for 0% -> 0%
where the time goes in v1:
time: 177 us; the launch traced here: 176 us
  Pallas kernels  162 us (92%)
  other arithmetic  9.62 us (5%)
  local copies, waits for them, and re-layouts  3.48 us (2%)
    pallas_call x1, Pallas kernels, run_train(): pl.pallas_call(functools.partial(train_kernel, cfg), out_shape=(jax.Shape...  162 us
    convert_element_type x1, other arithmetic, on_device(): frames.astype(F32)  4.34 us
    convert_element_type x4, other arithmetic, adamw_update(): return (updated, new_moment, new_square, updated.astype(BF))  3.93 us

profile of v1, /device:TPU:0, one launch (start us, length us, event | category | flops | bytes accessed | tf_op | source)
XLA Modules:
  0.0 176.4 jit_solution(13086729545727519399)
XLA Ops:
  0.7 0.7 tile.4
  1.3 0.1 tile.10
  1.4 0.5 compare_select_fusion.refs_7_
  1.9 162.5 %shard_map.312 = (bf16[2,2,512,512]{3,2,1,0:T(8,128)(2,1)}, bf16[2,256,256]{2,1,0:T(8,128)(2,1)}, f32[3,8,384]{2,1,0:T(8,128)}, f32[1536,128]{1,0:T(8,128)}, f32[256,128]{1,0:T(8,128)}) custom-call(bf16[2,256,512]{2,1,0:T(8,128)(2,1)} %bitcast.30, bf16[2,2,128]{2,1,0:T(2,128)(2,1)} %refs_1_.1, s32[2,2,512]{2,1,0:T(2,128)} %refs_2_.1, s32[2,2]{1,0:T(2,128)} %refs_3_.1, ...), custom_call_target="tpu_custom_call" | custom-call | tf_op jit(solution)/shard_map/pallas_call | solution.py:943
  164.4 0.0 copy-start
  164.4 0.0 copy-start.1
  164.4 0.0 copy-start.2
  164.5 0.0 copy-start.3
  164.5 4.3 %convert_element_type.21 = f32[2,2,512,512]{3,2,1,0:T(8,128)} convert(bf16[2,2,512,512]{3,2,1,0:T(8,128)(2,1)} %get-tuple-element.24) | non-fusion elementwise | flops 1048576 | bytes 6291456 | tf_op jit(solution)/shard_map/convert_element_type | solution.py:1029
  168.8 0.0 copy-done
  168.8 0.0 copy-done.1
  168.8 0.0 copy-done.2
  168.8 0.0 copy-done.3
  168.8 0.0 copy-start.5
  168.8 0.0 copy-start.4
  168.8 0.0 copy-start.6
  168.9 0.0 copy-start.7
  168.9 0.0 copy-start.8
  168.9 0.0 copy-start.12
  168.9 0.0 copy-start.13
  168.9 0.0 copy-start.14
  168.9 0.0 copy-start.9
  168.9 0.0 copy-start.10
  168.9 0.0 copy-start.11
  169.0 1.9 %fusion.15 = (bf16[196608]{0:T(1024)(128)(2,1)}, f32[196608]{0:T(1024)}, f32[196608]{0:T(1024)}, f32[196608]{0:T(1024)}) fusion(f32[196608]{0:T(1024)S(1)} %copy-done, f32[1536,128]{1,0:T(8,128)S(1)} %copy-done.3, f32[196608]{0:T(1024)S(1)} %copy-done.1, f32[196608]{0:T(1024)S(1)} %copy-done.2), kind=kLoop, calls=%fused_computation.29 | loop fusion | flops 3145728 | bytes 5898240 | tf_op jit(solution)/shard_map/convert_element_type | solution.py:970
  170.9 0.0 copy-done.5
  170.9 0.8 bitcast_convert_fusion
  171.7 0.0 copy-done.4
  171.7 0.0 copy-done.6
  171.7 0.0 copy-done.7
  171.7 0.0 copy-done.8
  171.7 0.8 fusion.9
  172.5 0.7 slice.10
  173.2 0.0 copy-done.12
  173.2 0.0 copy-done.13
  173.2 0.0 copy-done.14
  173.2 0.6 fusion.12
  173.8 0.7 slice.11
  174.5 0.0 copy-done.9
  174.5 0.0 copy-done.10
  174.5 0.0 copy-done.11
  174.5 0.6 fusion.7
  175.1 1.3 slice.9
Async XLA Ops:
  164.4 4.4 %copy-start = (f32[196608]{0:T(1024)S(1)}, f32[196608]{0:T(1024)}, u32[]{:S(2)}) copy-start(f32[196608]{0:T(1024)} %param.22) | copy-start | bytes 2359300
  164.4 4.4 %copy-start.1 = (f32[196608]{0:T(1024)S(1)}, f32[196608]{0:T(1024)}, u32[]{:S(2)}) copy-start(f32[196608]{0:T(1024)} %param.24) | copy-start | bytes 2359300
  164.4 4.4 %copy-start.2 = (f32[196608]{0:T(1024)S(1)}, f32[196608]{0:T(1024)}, u32[]{:S(2)}) copy-start(f32[196608]{0:T(1024)} %param.23) | copy-start | bytes 2359300
  164.5 4.4 %copy-start.3 = (f32[1536,128]{1,0:T(8,128)S(1)}, f32[1536,128]{1,0:T(8,128)}, u32[]{:S(2)}) copy-start(f32[1536,128]{1,0:T(8,128)} %get-tuple-element.27) | copy-start | bytes 2359300
  168.8 2.0 %copy-start.5 = (bf16[2,256,256]{2,1,0:T(8,128)(2,1)S(1)}, bf16[2,256,256]{2,1,0:T(8,128)(2,1)}, u32[]{:S(2)}) copy-start(bf16[2,256,256]{2,1,0:T(8,128)(2,1)} %get-tuple-element.25) | copy-start | bytes 786436
  168.8 2.9 %copy-start.4 = (f32[32768]{0:T(1024)S(1)}, f32[32768]{0:T(1024)}, u32[]{:S(2)}) copy-start(f32[32768]{0:T(1024)} %param.28) | copy-start | bytes 393220
  168.8 2.8 %copy-start.6 = (f32[32768]{0:T(1024)S(1)}, f32[32768]{0:T(1024)}, u32[]{:S(2)}) copy-start(f32[32768]{0:T(1024)} %param.30) | copy-start | bytes 393220
  168.9 2.8 %copy-start.7 = (f32[32768]{0:T(1024)S(1)}, f32[32768]{0:T(1024)}, u32[]{:S(2)}) copy-start(f32[32768]{0:T(1024)} %param.29) | copy-start | bytes 393220
  168.9 2.8 %copy-start.8 = (f32[256,128]{1,0:T(8,128)S(1)}, f32[256,128]{1,0:T(8,128)}, u32[]{:S(2)}) copy-start(f32[256,128]{1,0:T(8,128)} %get-tuple-element.28) | copy-start | bytes 393220
  168.9 4.3 %copy-start.12 = (f32[64]{0:T(128)S(1)}, f32[64]{0:T(128)}, u32[]{:S(2)}) copy-start(f32[64]{0:T(128)} %param.25) | copy-start | bytes 772
  168.9 4.3 %copy-start.13 = (f32[64]{0:T(128)S(1)}, f32[64]{0:T(128)}, u32[]{:S(2)}) copy-start(f32[64]{0:T(128)} %param.27) | copy-start | bytes 772
  168.9 4.3 %copy-start.14 = (f32[64]{0:T(128)S(1)}, f32[64]{0:T(128)}, u32[]{:S(2)}) copy-start(f32[64]{0:T(128)} %param.26) | copy-start | bytes 772
  168.9 5.6 %copy-start.9 = (f32[256]{0:T(256)S(1)}, f32[256]{0:T(256)}, u32[]{:S(2)}) copy-start(f32[256]{0:T(256)} %param.31) | copy-start | bytes 3076
  168.9 5.6 %copy-start.10 = (f32[256]{0:T(256)S(1)}, f32[256]{0:T(256)}, u32[]{:S(2)}) copy-start(f32[256]{0:T(256)} %param.33) | copy-start | bytes 3076
  168.9 5.6 %copy-start.11 = (f32[256]{0:T(256)S(1)}, f32[256]{0:T(256)}, u32[]{:S(2)}) copy-start(f32[256]{0:T(256)} %param.32) | copy-start | bytes 3076
